TPU v7x, 32 devices: a whole 2x2x4 slice. The times are simulated.
32 devices in a mesh: wall: 2 (over x), span: 4 (over y, core), chord: 4 (over z).
Axes of the slice: x: 2, y: 2, z: 4, core: 2. Of those that a mesh axis runs over, the one named last changes fastest.
Arguments:
- source: float32 [4, 8, 8, 4, 320], P('span', 'chord', 'wall'), may hold values from -1.8 to 1.8
- adjoint_start: float32 [4, 8, 8, 4, 320], P('span', 'chord', 'wall'), may hold values from -6 to 6
- pivot_inverse: float32 [4, 8, 8, 320, 320], P('span', 'chord', 'wall'), as said below
- upper_block: float32 [4, 8, 8, 320, 320], P('span', 'chord', 'wall'), may hold values from -0.3125 to 0.3125
- lower_block: float32 [4, 8, 8, 320, 320], P('span', 'chord', 'wall'), may hold values from -0.3125 to 0.3125
- face_coupling: float32 [4, 80, 320], replicated, may hold values from -0.03125 to 0.03125
Outputs:
- adjoint: float32 [4, 8, 8, 4, 320], P('span', 'chord', 'wall')
Inputs may be any that keep to these rules, and one draw needn't show every extreme that they name: `pivot_inverse`: each block equals 0.9 times the identity plus independent noise of root-mean-square 0.3 times 320 ** -0.5 an entry.
All inputs are finite; a program needn't handle non-finite values.
Results may differ from a plain program's by a relative error of at most 0.0003.
Values sent between devices are 32-bit elements; how exact they have to be, the bound alone decides.
A program may use at most 128 MiB of HBM per device.

v0:
```python
import functools
import jax
import jax.numpy as jnp
from jax import lax
from jax.experimental import pallas as pl
from jax.experimental.pallas import tpu as pltpu
from jax.sharding import PartitionSpec as P

NV = 5
P1 = 4
SWEEPS = 2
AXES = ("wall", "span", "chord")


def kernel(sizes, src, adj, piv, upp, low, face, out,
           wf, wh, wl, ef, eh, el, zs, rs, fw, ab, sf, sb, rf, rb,
           r_sn, r_sp, r_cn, r_cp, msem, wsend, wrecv, fsend, frecv):
    lines, elements, obj, width = src.shape[1:]
    rows = lines * elements * obj
    place = {a: lax.axis_index(a) for a in AXES}
    f32, bf16 = jnp.float32, jnp.bfloat16

    def has(axis, step):
        return place[axis] < sizes[axis] - 1 if step > 0 else place[axis] > 0

    def to(axis, step):
        return {axis: jnp.clip(place[axis] + step, 0, sizes[axis] - 1)}

    def load(kind, ref, e):
        return pltpu.make_async_copy(ref.at[0, :, e], wf.at[kind, e], msem.at[kind, e])

    for e in range(elements):
        load(0, piv, e).start()
        load(1, upp, e).start()
    for e in reversed(range(elements)):
        load(2, low, e).start()

    barrier = pltpu.get_barrier_semaphore()
    sides = [(a, s) for a in AXES for s in (1, -1)]
    for axis, step in sides:
        @pl.when(has(axis, step))
        def _():
            pl.semaphore_signal(barrier, inc=1, device_id=to(axis, step), device_id_type=pl.DeviceIdType.MESH)
    pl.semaphore_wait(barrier, sum(has(axis, step).astype(jnp.int32) for axis, step in sides))

    def face_copies(sweep):
        whole = adj.at[0] if sweep == 0 else ab
        parts = (
            ("span", -1, whole, r_sn),
            ("span", 1, whole, r_sp),
            ("chord", -1, whole.at[0], r_cn),
            ("chord", 1, whole.at[lines - 1], r_cp),
        )
        return [
            (axis, step, pltpu.make_async_remote_copy(
                src_ref=a, dst_ref=b.at[sweep], send_sem=fsend.at[sweep, i], recv_sem=frecv.at[sweep, i],
                device_id=to(axis, step), device_id_type=pl.DeviceIdType.MESH))
            for i, (axis, step, a, b) in enumerate(parts)
        ]

    def send_faces(sweep):
        for axis, step, copy in face_copies(sweep):
            @pl.when(has(axis, step))
            def _():
                copy.start()

    def wait_faces(sweep):
        for axis, step, copy in face_copies(sweep):
            @pl.when(has(axis, -step))
            def _():
                copy.wait_recv()

    def wall_copy(sweep, way):
        a, b = (sf, rf) if way > 0 else (sb, rb)
        i = 0 if way > 0 else 1
        return pltpu.make_async_remote_copy(
            src_ref=a.at[sweep], dst_ref=b.at[sweep], send_sem=wsend.at[sweep, i], recv_sem=wrecv.at[sweep, i],
            device_id=to("wall", way), device_id_type=pl.DeviceIdType.MESH)

    def split_block(kind, ref, e):
        load(kind, ref, e).wait()
        for line in range(lines):
            full = wf[kind, e, line]
            high = full.astype(bf16)
            wh[kind, e, line] = high
            wl[kind, e, line] = (full - high.astype(f32)).astype(bf16)

    def pieces(x):
        high = x.astype(bf16).astype(f32)
        return jnp.concatenate([high, x - high], axis=0).astype(bf16)

    def times(x, high, low_):
        n = x.shape[0]
        both = pieces(x)
        y = jnp.dot(both, high, preferred_element_type=f32) + jnp.dot(both, low_, preferred_element_type=f32)
        return y[:n] + y[n:]

    send_faces(0)

    for axis, step, ref in (("span", 1, r_sn), ("span", -1, r_sp), ("chord", 1, r_cn), ("chord", -1, r_cp)):
        @pl.when(jnp.logical_not(has(axis, step)))
        def _():
            ref[...] = jnp.zeros_like(ref)

    @pl.when(jnp.logical_not(has("wall", -1)))
    def _():
        rf[...] = jnp.zeros_like(rf)

    @pl.when(jnp.logical_not(has("wall", 1)))
    def _():
        rb[...] = jnp.zeros_like(rb)

    ef[...] = jnp.zeros_like(ef)
    run = P1 * P1
    for v in range(NV):
        top = v * P1 * run
        ef[0, top:top + run, :] = face[0, v * run:(v + 1) * run, :]
        ef[0, top + 3 * run:top + 4 * run, :] = face[1, v * run:(v + 1) * run, :]
    for g in range(NV * P1):
        ef[1, g * run:g * run + P1, :] = face[2, g * P1:(g + 1) * P1, :]
        ef[1, g * run + 3 * P1:(g + 1) * run, :] = face[3, g * P1:(g + 1) * P1, :]
    for d in range(2):
        full = ef[d]
        high = full.astype(bf16)
        eh[d] = high
        el[d] = (full - high.astype(f32)).astype(bf16)

    for e in range(elements):
        split_block(0, piv, e)
        split_block(1, upp, e)

    lane = lax.broadcasted_iota(jnp.int32, (obj, width), 1)
    span_node = (lane >> 4) & 3
    chord_node = (lane >> 2) & 3

    for sweep in range(SWEEPS):
        wait_faces(sweep)
        for line in range(lines):
            for e in range(elements):
                at = (line * elements + e) * obj
                now = adj.at[0] if sweep == 0 else ab
                zs[0, at:at + obj, :] = jnp.where(
                    span_node == 0, r_sn[sweep, line, e], jnp.where(span_node == 3, r_sp[sweep, line, e], 0.0))
                above = now[line + 1, e] if line + 1 < lines else r_cn[sweep, e]
                below = now[line - 1, e] if line > 0 else r_cp[sweep, e]
                zs[1, at:at + obj, :] = jnp.where(
                    chord_node == 0, above, jnp.where(chord_node == 3, below, 0.0))
        rs[...] = times(zs[0], eh[0], el[0]) + times(zs[1], eh[1], el[1])

        if sweep == 0:
            @pl.when(has("wall", -1))
            def _():
                for e in reversed(range(elements)):
                    split_block(2, low, e)

        @pl.when(has("wall", -1))
        def _():
            wall_copy(sweep, 1).wait_recv()

        carried = [rf[sweep, line] for line in range(lines)]
        for e in range(elements):
            for line in range(lines):
                at = (line * elements + e) * obj
                value = times(src[0, line, e] - rs[at:at + obj, :] - carried[line], wh[0, e, line], wl[0, e, line])
                fw[line, e] = value
                carried[line] = times(value, wh[1, e, line], wl[1, e, line])
        for line in range(lines):
            sf[sweep, line] = carried[line]

        @pl.when(has("wall", 1))
        def _():
            wall_copy(sweep, 1).start()

        if sweep == 0:
            @pl.when(jnp.logical_not(has("wall", -1)))
            def _():
                for e in reversed(range(elements)):
                    split_block(2, low, e)

        @pl.when(has("wall", 1))
        def _():
            wall_copy(sweep, -1).wait_recv()

        last = sweep == SWEEPS - 1
        carried = [rb[sweep, line] for line in range(lines)]
        for e in reversed(range(elements)):
            for line in range(lines):
                value = fw[line, e] - carried[line]
                if last:
                    out[0, line, e] = value
                else:
                    ab[line, e] = value
                carried[line] = times(value, wh[2, e, line], wl[2, e, line])
        for line in range(lines):
            sb[sweep, line] = carried[line]

        @pl.when(has("wall", -1))
        def _():
            wall_copy(sweep, -1).start()

        if not last:
            send_faces(sweep + 1)

    for sweep in range(SWEEPS):
        for axis, step, copy in face_copies(sweep):
            @pl.when(has(axis, step))
            def _():
                copy.wait_send()
        for way in (1, -1):
            @pl.when(has("wall", way))
            def _():
                wall_copy(sweep, way).wait_send()


def local(sizes, source, adjoint_start, pivot_inverse, upper_block, lower_block, face_coupling):
    lines, elements, obj, width = source.shape[1:]
    f32, bf16 = jnp.float32, jnp.bfloat16
    vmem = pl.BlockSpec(memory_space=pltpu.VMEM)
    anywhere = pl.BlockSpec(memory_space=pl.ANY)
    rows = lines * elements * obj
    edge = pltpu.VMEM((SWEEPS, lines, obj, width), f32)
    blocks = (3, elements, lines, width, width)
    return pl.pallas_call(
        functools.partial(kernel, sizes),
        out_shape=jax.ShapeDtypeStruct(source.shape, f32),
        in_specs=[vmem, vmem, anywhere, anywhere, anywhere, vmem],
        out_specs=vmem,
        scratch_shapes=[
            pltpu.VMEM(blocks, f32), pltpu.VMEM(blocks, bf16), pltpu.VMEM(blocks, bf16),
            pltpu.VMEM((2, width, width), f32), pltpu.VMEM((2, width, width), bf16),
            pltpu.VMEM((2, width, width), bf16),
            pltpu.VMEM((2, rows, width), f32), pltpu.VMEM((rows, width), f32),
            pltpu.VMEM((lines, elements, obj, width), f32), pltpu.VMEM((lines, elements, obj, width), f32),
            edge, edge, edge, edge,
            pltpu.VMEM((SWEEPS, lines, elements, obj, width), f32),
            pltpu.VMEM((SWEEPS, lines, elements, obj, width), f32),
            pltpu.VMEM((SWEEPS, elements, obj, width), f32),
            pltpu.VMEM((SWEEPS, elements, obj, width), f32),
            pltpu.SemaphoreType.DMA((3, elements)),
            pltpu.SemaphoreType.DMA((SWEEPS, 2)), pltpu.SemaphoreType.DMA((SWEEPS, 2)),
            pltpu.SemaphoreType.DMA((SWEEPS, 4)), pltpu.SemaphoreType.DMA((SWEEPS, 4)),
        ],
        compiler_params=pltpu.CompilerParams(
            collective_id=0, has_side_effects=True, vmem_limit_bytes=60 * 1024 * 1024),
    )(source, adjoint_start, pivot_inverse, upper_block, lower_block, face_coupling)


def solution(mesh):
    spec = P("span", "chord", "wall", None, None)
    return jax.shard_map(
        functools.partial(local, dict(mesh.shape)),
        mesh=mesh,
        in_specs=(spec, spec, spec, spec, spec, P()),
        out_specs=spec,
        check_vma=False,
    )
```

profile of v0, /device:TPU:0, one launch (start us, length us, event | category | flops | bytes accessed | tf_op | source)
XLA Modules:
  0.0 36.5 jit_solution(13556015314003738601)
XLA Ops:
  0.0 35.0 %shard_map.64 = f32[1,2,4,4,320]{4,3,2,1,0:T(4,128)} custom-call(f32[1,2,4,4,320]{4,3,2,1,0:T(4,128)} %src.1, f32[1,2,4,4,320]{4,3,2,1,0:T(4,128)} %adj.1, f32[1,2,4,320,320]{4,3,2,1,0:T(8,128)} %piv.1, f32[1,2,4,320,320]{4,3,2,1,0:T(8,128)} %upp.1, f32[1,2,4,320,320]{4,3,2,1,0:T(8,128)} %low.1, f32[4,80,320]{2,1,0:T(8,128)} %face.1), custom_call_target="tpu_custom_call" | custom-call | tf_op jit(solution)/shard_map/pallas_call | solution.py:223
  35.0 1.4 %copy.8 = f32[1,2,4,4,320]{4,3,2,1,0:T(4,128)} copy(f32[1,2,4,4,320]{4,3,2,1,0:T(4,128)} %shard_map.64) | data formatting | bytes 81920
where the time goes:
time: 36.6 us; the launch traced here: 36.5 us
  Pallas kernels  35 us (96%)
  local copies, waits for them, and re-layouts  1.42 us (4%)
    pallas_call x1, Pallas kernels, local(): pl.pallas_call(functools.partial(kernel, sizes), out_shape=jax.ShapeDtype...  35 us
    unnamed x1, local copies, waits for them, and re-layouts  1.42 us

commit v1 on v0

--- a/solution.py
+++ b/solution.py
@@ -12,10 +12,10 @@
 AXES = ("wall", "span", "chord")
 
 
-def kernel(sizes, src, adj, piv, upp, low, face, out,
-           wf, wh, wl, ef, eh, el, zs, rs, fw, ab, sf, sb, rf, rb,
+def kernel(sizes, src_in, adj_in, piv, upp, low, face_in, out,
+           src, adj, face, qh, ql, th, tl, small, wf, wh, wl, ef, eh, el, zs, rs, fw, ab, sf, sb, rf, rb,
            r_sn, r_sp, r_cn, r_cp, msem, wsend, wrecv, fsend, frecv):
-    lines, elements, obj, width = src.shape[1:]
+    lines, elements, obj, width = src_in.shape[1:]
     rows = lines * elements * obj
     place = {a: lax.axis_index(a) for a in AXES}
     f32, bf16 = jnp.float32, jnp.bfloat16
@@ -29,6 +29,12 @@
     def load(kind, ref, e):
         return pltpu.make_async_copy(ref.at[0, :, e], wf.at[kind, e], msem.at[kind, e])
 
+    minor = [
+        pltpu.make_async_copy(a, b, small.at[i])
+        for i, (a, b) in enumerate(((face_in, face), (adj_in, adj), (src_in, src)))
+    ]
+    for copy in minor:
+        copy.start()
     for e in range(elements):
         load(0, piv, e).start()
         load(1, upp, e).start()
@@ -43,29 +49,32 @@
             pl.semaphore_signal(barrier, inc=1, device_id=to(axis, step), device_id_type=pl.DeviceIdType.MESH)
     pl.semaphore_wait(barrier, sum(has(axis, step).astype(jnp.int32) for axis, step in sides))
 
-    def face_copies(sweep):
-        whole = adj.at[0] if sweep == 0 else ab
-        parts = (
-            ("span", -1, whole, r_sn),
-            ("span", 1, whole, r_sp),
-            ("chord", -1, whole.at[0], r_cn),
-            ("chord", 1, whole.at[lines - 1], r_cp),
-        )
-        return [
-            (axis, step, pltpu.make_async_remote_copy(
-                src_ref=a, dst_ref=b.at[sweep], send_sem=fsend.at[sweep, i], recv_sem=frecv.at[sweep, i],
-                device_id=to(axis, step), device_id_type=pl.DeviceIdType.MESH))
-            for i, (axis, step, a, b) in enumerate(parts)
-        ]
-
-    def send_faces(sweep):
-        for axis, step, copy in face_copies(sweep):
+    def face_copies(sweep, which=(0, 1)):
+        whole = adj_in.at[0] if sweep == 0 else ab
+        found = []
+        for part, cut in enumerate((pl.ds(1, elements - 1), pl.ds(0, 1))):
+            if part not in which:
+                continue
+            parts = (
+                ("chord", -1, whole.at[0, cut], r_cn.at[sweep, cut]),
+                ("chord", 1, whole.at[lines - 1, cut], r_cp.at[sweep, cut]),
+                ("span", -1, whole.at[:, cut], r_sn.at[sweep, :, cut]),
+                ("span", 1, whole.at[:, cut], r_sp.at[sweep, :, cut]),
+            )
+            for i, (axis, step, a, b) in enumerate(parts):
+                found.append((part, axis, step, pltpu.make_async_remote_copy(
+                    src_ref=a, dst_ref=b, send_sem=fsend.at[sweep, part, i], recv_sem=frecv.at[sweep, part, i],
+                    device_id=to(axis, step), device_id_type=pl.DeviceIdType.MESH)))
+        return found
+
+    def send_faces(sweep, which):
+        for part, axis, step, copy in face_copies(sweep, (which,)):
             @pl.when(has(axis, step))
             def _():
                 copy.start()
 
     def wait_faces(sweep):
-        for axis, step, copy in face_copies(sweep):
+        for part, axis, step, copy in face_copies(sweep):
             @pl.when(has(axis, -step))
             def _():
                 copy.wait_recv()
@@ -95,7 +104,38 @@
         y = jnp.dot(both, high, preferred_element_type=f32) + jnp.dot(both, low_, preferred_element_type=f32)
         return y[:n] + y[n:]
 
-    send_faces(0)
+    def product(ah, al, bh, bl):
+        dot = functools.partial(jnp.dot, preferred_element_type=f32)
+        return dot(ah, bh) + dot(al, bh) + dot(ah, bl)
+
+    def halves(full):
+        high = full.astype(bf16)
+        return high, (full - high.astype(f32)).astype(bf16)
+
+    def form_pairs(line, unused):
+        for e in range(elements):
+            qh[e, line], ql[e, line] = halves(
+                product(wh[0, e, line], wl[0, e, line], wh[1, e, line], wl[1, e, line]))
+        return unused
+
+    start = 1 if elements > 1 else 0
+
+    def begin_response(line, unused):
+        e = elements - 1
+        th[line], tl[line] = halves(-product(wh[0, e, line], wl[0, e, line], wh[2, e, line], wl[2, e, line]))
+        return unused
+
+    def form_response(line, unused):
+        eye = (lax.broadcasted_iota(jnp.int32, (width, width), 0)
+               == lax.broadcasted_iota(jnp.int32, (width, width), 1)).astype(f32)
+        for e in reversed(range(start, elements - 1)):
+            ah, al = halves(eye - product(wh[1, e, line], wl[1, e, line], th[line], tl[line]))
+            ah, al = halves(product(wh[0, e, line], wl[0, e, line], ah, al))
+            th[line], tl[line] = halves(-product(ah, al, wh[2, e, line], wl[2, e, line]))
+        return unused
+
+    send_faces(0, 0)
+    send_faces(0, 1)
 
     for axis, step, ref in (("span", 1, r_sn), ("span", -1, r_sp), ("chord", 1, r_cn), ("chord", -1, r_cp)):
         @pl.when(jnp.logical_not(has(axis, step)))
@@ -111,6 +151,7 @@
         rb[...] = jnp.zeros_like(rb)
 
     ef[...] = jnp.zeros_like(ef)
+    minor[0].wait()
     run = P1 * P1
     for v in range(NV):
         top = v * P1 * run
@@ -129,6 +170,9 @@
         split_block(0, piv, e)
         split_block(1, upp, e)
 
+    minor[1].wait()
+    minor[2].wait()
+
     lane = lax.broadcasted_iota(jnp.int32, (obj, width), 1)
     span_node = (lane >> 4) & 3
     chord_node = (lane >> 2) & 3
@@ -147,62 +191,127 @@
                     chord_node == 0, above, jnp.where(chord_node == 3, below, 0.0))
         rs[...] = times(zs[0], eh[0], el[0]) + times(zs[1], eh[1], el[1])
 
-        if sweep == 0:
-            @pl.when(has("wall", -1))
-            def _():
-                for e in reversed(range(elements)):
-                    split_block(2, low, e)
-
-        @pl.when(has("wall", -1))
-        def _():
+        last = sweep == SWEEPS - 1
+
+        def right(line, e):
+            at = (line * elements + e) * obj
+            return src[0, line, e] - rs[at:at + obj, :]
+
+        def forward(carried, final=True, first=0, end=elements):
+            carried = list(carried)
+            for e in range(first, end):
+                for line in range(lines):
+                    value = times(right(line, e) - carried[line], wh[0, e, line], wl[0, e, line])
+                    fw[line, e] = value
+                    if final or e < end - 1:
+                        carried[line] = times(value, wh[1, e, line], wl[1, e, line])
+            return carried
+
+        def backward(carried, store, final=True, first=0, end=elements):
+            carried = list(carried)
+            for e in reversed(range(first, end)):
+                for line in range(lines):
+                    value = fw[line, e] - carried[line]
+                    if store:
+                        if last:
+                            out[0, line, e] = value
+                        else:
+                            ab[line, e] = value
+                    if final or e > first:
+                        carried[line] = times(value, wh[2, e, line], wl[2, e, line])
+                if store and not last and e == 1:
+                    send_faces(sweep + 1, 0)
+            return carried
+
+        def received(ref):
+            return [ref[sweep, line] for line in range(lines)]
+
+        def keep(ref, values):
+            for line in range(lines):
+                ref[sweep, line] = values[line]
+
+        blank = [jnp.zeros((obj, width), f32)] * lines
+        opening, closing = jnp.logical_not(has("wall", -1)), jnp.logical_not(has("wall", 1))
+        middle = jnp.logical_and(has("wall", -1), has("wall", 1))
+
+        def split_lower():
+            for e in reversed(range(elements)):
+                split_block(2, low, e)
+
+        @pl.when(opening)
+        def _():
+            if sweep == 0:
+                keep(sf, forward(blank))
+            else:
+                carried = list(blank)
+                for e in range(elements):
+                    for line in range(lines):
+                        small_right = right(line, e) - carried[line]
+                        rs[(line * elements + e) * obj:(line * elements + e + 1) * obj, :] = small_right
+                        carried[line] = times(small_right, qh[e, line], ql[e, line])
+                keep(sf, carried)
+
+            @pl.when(has("wall", 1))
+            def _():
+                wall_copy(sweep, 1).start()
+
+            if sweep == 0:
+                split_lower()
+                lax.fori_loop(0, lines, form_pairs, 0)
+            else:
+                for e in range(elements):
+                    for line in range(lines):
+                        at = (line * elements + e) * obj
+                        fw[line, e] = times(rs[at:at + obj, :], wh[0, e, line], wl[0, e, line])
+
+            @pl.when(has("wall", 1))
+            def _():
+                wall_copy(sweep, -1).wait_recv()
+
+            backward(received(rb), True, False)
+            if not last:
+                send_faces(sweep + 1, 1)
+
+        @pl.when(middle)
+        def _():
+            if sweep == 0:
+                split_lower()
             wall_copy(sweep, 1).wait_recv()
-
-        carried = [rf[sweep, line] for line in range(lines)]
-        for e in range(elements):
-            for line in range(lines):
-                at = (line * elements + e) * obj
-                value = times(src[0, line, e] - rs[at:at + obj, :] - carried[line], wh[0, e, line], wl[0, e, line])
-                fw[line, e] = value
-                carried[line] = times(value, wh[1, e, line], wl[1, e, line])
-        for line in range(lines):
-            sf[sweep, line] = carried[line]
-
-        @pl.when(has("wall", 1))
-        def _():
+            keep(sf, forward(received(rf)))
             wall_copy(sweep, 1).start()
-
-        if sweep == 0:
-            @pl.when(jnp.logical_not(has("wall", -1)))
-            def _():
-                for e in reversed(range(elements)):
-                    split_block(2, low, e)
-
-        @pl.when(has("wall", 1))
-        def _():
             wall_copy(sweep, -1).wait_recv()
-
-        last = sweep == SWEEPS - 1
-        carried = [rb[sweep, line] for line in range(lines)]
-        for e in reversed(range(elements)):
-            for line in range(lines):
-                value = fw[line, e] - carried[line]
-                if last:
-                    out[0, line, e] = value
-                else:
-                    ab[line, e] = value
-                carried[line] = times(value, wh[2, e, line], wl[2, e, line])
-        for line in range(lines):
-            sb[sweep, line] = carried[line]
-
-        @pl.when(has("wall", -1))
-        def _():
+            keep(sb, backward(received(rb), True))
             wall_copy(sweep, -1).start()
-
-        if not last:
-            send_faces(sweep + 1)
+            if not last:
+                send_faces(sweep + 1, 1)
+
+        @pl.when(jnp.logical_and(closing, has("wall", -1)))
+        def _():
+            if sweep == 0:
+                split_lower()
+                lax.fori_loop(0, lines, begin_response, 0)
+                wall_copy(sweep, 1).wait_recv()
+                forward(received(rf), False)
+                keep(sb, backward(blank, True))
+                wall_copy(sweep, -1).start()
+                if not last:
+                    send_faces(sweep + 1, 1)
+                    lax.fori_loop(0, lines, form_response, 0)
+            else:
+                forward(blank, False, start)
+                apart = backward(blank, False, True, start)
+                wall_copy(sweep, 1).wait_recv()
+                came = forward(received(rf), True, 0, start)
+                back = [apart[line] + times(came[line], th[line], tl[line]) for line in range(lines)]
+                keep(sb, backward(back, True, True, 0, start))
+                wall_copy(sweep, -1).start()
+                forward(came, False, start)
+                backward(blank, True, False, start)
+                if not last:
+                    send_faces(sweep + 1, 1)
 
     for sweep in range(SWEEPS):
-        for axis, step, copy in face_copies(sweep):
+        for part, axis, step, copy in face_copies(sweep):
             @pl.when(has(axis, step))
             def _():
                 copy.wait_send()
@@ -223,9 +332,12 @@
     return pl.pallas_call(
         functools.partial(kernel, sizes),
         out_shape=jax.ShapeDtypeStruct(source.shape, f32),
-        in_specs=[vmem, vmem, anywhere, anywhere, anywhere, vmem],
+        in_specs=[anywhere] * 6,
         out_specs=vmem,
         scratch_shapes=[
+            pltpu.VMEM(source.shape, f32), pltpu.VMEM(source.shape, f32), pltpu.VMEM(face_coupling.shape, f32),
+            pltpu.VMEM(blocks[1:], bf16), pltpu.VMEM(blocks[1:], bf16),
+            pltpu.VMEM(blocks[2:], bf16), pltpu.VMEM(blocks[2:], bf16), pltpu.SemaphoreType.DMA((3,)),
             pltpu.VMEM(blocks, f32), pltpu.VMEM(blocks, bf16), pltpu.VMEM(blocks, bf16),
             pltpu.VMEM((2, width, width), f32), pltpu.VMEM((2, width, width), bf16),
             pltpu.VMEM((2, width, width), bf16),
@@ -238,7 +350,7 @@
             pltpu.VMEM((SWEEPS, elements, obj, width), f32),
             pltpu.SemaphoreType.DMA((3, elements)),
             pltpu.SemaphoreType.DMA((SWEEPS, 2)), pltpu.SemaphoreType.DMA((SWEEPS, 2)),
-            pltpu.SemaphoreType.DMA((SWEEPS, 4)), pltpu.SemaphoreType.DMA((SWEEPS, 4)),
+            pltpu.SemaphoreType.DMA((SWEEPS, 2, 4)), pltpu.SemaphoreType.DMA((SWEEPS, 2, 4)),
         ],
         compiler_params=pltpu.CompilerParams(
             collective_id=0, has_side_effects=True, vmem_limit_bytes=60 * 1024 * 1024),

time: 36.6 us -> 31.9 us (0.87)
  Pallas kernels: 35 us -> 30.3 us
    pallas_call x1, Pallas kernels: 35 us -> 30.3 us  [local(): pl.pallas_call(functools.partial(kernel, sizes), out_shape=jax.ShapeDtype...]
where the time goes in v1:
time: 31.9 us; the launch traced here: 31.8 us
  Pallas kernels  30.3 us (95%)
  local copies, waits for them, and re-layouts  1.42 us (4%)
    pallas_call x1, Pallas kernels, local(): pl.pallas_call(functools.partial(kernel, sizes), out_shape=jax.ShapeDtype...  30.3 us
    unnamed x1, local copies, waits for them, and re-layouts  1.42 us

profile of v1, /device:TPU:0, one launch (start us, length us, event | category | flops | bytes accessed | tf_op | source)
XLA Modules:
  0.0 31.8 jit_solution(2840692759932619738)
XLA Ops:
  0.0 30.3 %shard_map.64 = f32[1,2,4,4,320]{4,3,2,1,0:T(4,128)} custom-call(f32[1,2,4,4,320]{4,3,2,1,0:T(4,128)} %src_in.1, f32[1,2,4,4,320]{4,3,2,1,0:T(4,128)} %adj_in.1, f32[1,2,4,320,320]{4,3,2,1,0:T(8,128)} %piv.1, f32[1,2,4,320,320]{4,3,2,1,0:T(8,128)} %upp.1, f32[1,2,4,320,320]{4,3,2,1,0:T(8,128)} %low.1, f32[4,80,320]{2,1,0:T(8,128)} %face_in.1), custom_call_target="tpu_custom_call" | custom-call | tf_op jit(solution)/shard_map/pallas_call | solution.py:332
  30.3 1.4 %copy.8 = f32[1,2,4,4,320]{4,3,2,1,0:T(4,128)} copy(f32[1,2,4,4,320]{4,3,2,1,0:T(4,128)} %shard_map.64) | data formatting | bytes 81920

commit v2 on v1

--- a/solution.py
+++ b/solution.py
@@ -207,7 +207,7 @@
                         carried[line] = times(value, wh[1, e, line], wl[1, e, line])
             return carried
 
-        def backward(carried, store, final=True, first=0, end=elements):
+        def backward(carried, store, final=True, first=0, end=elements, early=True):
             carried = list(carried)
             for e in reversed(range(first, end)):
                 for line in range(lines):
@@ -219,7 +219,7 @@
                             ab[line, e] = value
                     if final or e > first:
                         carried[line] = times(value, wh[2, e, line], wl[2, e, line])
-                if store and not last and e == 1:
+                if early and store and not last and e == 1:
                     send_faces(sweep + 1, 0)
             return carried
 
@@ -290,10 +290,18 @@
             if sweep == 0:
                 split_lower()
                 lax.fori_loop(0, lines, begin_response, 0)
+                tail = elements - 1
+                forward(blank, False, tail)
+                apart = backward(blank, False, True, tail)
                 wall_copy(sweep, 1).wait_recv()
-                forward(received(rf), False)
-                keep(sb, backward(blank, True))
+                came = forward(received(rf), True, 0, tail)
+                back = [apart[line] + times(came[line], th[line], tl[line]) for line in range(lines)]
+                keep(sb, backward(back, True, True, 0, tail, False))
                 wall_copy(sweep, -1).start()
+                forward(came, False, tail)
+                backward(blank, True, False, tail, elements, False)
+                if not last:
+                    send_faces(sweep + 1, 0)
                 if not last:
                     send_faces(sweep + 1, 1)
                     lax.fori_loop(0, lines, form_response, 0)

time: 31.9 us -> 32 us (level)
  no operation moved by 1% of the time
where the time goes in v2:
time: 32 us; the launch traced here: 31.8 us
  Pallas kernels  30.4 us (95%)
  local copies, waits for them, and re-layouts  1.42 us (4%)
    pallas_call x1, Pallas kernels, local(): pl.pallas_call(functools.partial(kernel, sizes), out_shape=jax.ShapeDtype...  30.4 us
    unnamed x1, local copies, waits for them, and re-layouts  1.42 us

profile of v2, /device:TPU:0, one launch (start us, length us, event | category | flops | bytes accessed | tf_op | source)
XLA Modules:
  0.0 31.8 jit_solution(3245315595102095659)
XLA Ops:
  0.0 30.4 %shard_map.64 = f32[1,2,4,4,320]{4,3,2,1,0:T(4,128)} custom-call(f32[1,2,4,4,320]{4,3,2,1,0:T(4,128)} %src_in.1, f32[1,2,4,4,320]{4,3,2,1,0:T(4,128)} %adj_in.1, f32[1,2,4,320,320]{4,3,2,1,0:T(8,128)} %piv.1, f32[1,2,4,320,320]{4,3,2,1,0:T(8,128)} %upp.1, f32[1,2,4,320,320]{4,3,2,1,0:T(8,128)} %low.1, f32[4,80,320]{2,1,0:T(8,128)} %face_in.1), custom_call_target="tpu_custom_call" | custom-call | tf_op jit(solution)/shard_map/pallas_call | solution.py:340
  30.4 1.4 %copy.8 = f32[1,2,4,4,320]{4,3,2,1,0:T(4,128)} copy(f32[1,2,4,4,320]{4,3,2,1,0:T(4,128)} %shard_map.64) | data formatting | bytes 81920
